TPU v7x, 32 devices: a whole 2x2x4 slice. The times are simulated.
32 devices in a mesh: dp: 4 (over z), expert: 4 (over y, core), mp: 2 (over x).
Axes of the slice: x: 2, y: 2, z: 4, core: 2. Of those that a mesh axis runs over, the one named last changes fastest.
Arguments:
- hidden: bfloat16 [2048, 2048], P(('dp', 'expert', 'mp')), may hold values from -6 to 6
- norm_gain: float32 [2048], replicated, may hold values from 0.1 to 1.9
- expert_in: float32 [16, 2048, 2816], P('dp', ('expert', 'mp')), may hold values from -0.125 to 0.125
- expert_out: float32 [16, 2048, 1408], P('dp', ('expert', 'mp')), may hold values from -0.15625 to 0.15625
- expert_ids: int32 [2048, 6], P(('dp', 'expert', 'mp')), may hold values from 0 to 15, all different within a row; in each aligned block of 64 rows (0 to 63, 64 to 127, ...) at most 48 rows name the same one
- gate_levels: int32 [2048, 6], P(('dp', 'expert', 'mp')), may hold values from 1 to 255
- shared_gate: bfloat16 [2048, 2816], P(('dp', 'expert'), 'mp'), may hold values from -0.125 to 0.125
- shared_up: bfloat16 [2048, 2816], P(('dp', 'expert'), 'mp'), may hold values from -0.125 to 0.125
- shared_down: bfloat16 [2048, 2816], P(('dp', 'expert'), 'mp'), may hold values from -0.109375 to 0.109375
- next_gain: float32 [2048], replicated, may hold values from 0.1 to 1.9
- kv_weight: bfloat16 [2048, 576], P(None, 'mp'), may hold values from -0.125 to 0.125
Outputs:
- layer_out: bfloat16 [2048, 2048], P(('dp', 'expert', 'mp'))
- kv_latent: bfloat16 [2048, 576], P(('dp', 'expert'), 'mp')
Inputs may be any that keep to these rules, and one draw needn't show every extreme that they name: `expert_ids`: each row names 6 different experts. Among the 64 rows of one device no expert is named by more than 48 rows, and in every draw some expert is named by exactly 48 rows of some device.
All inputs are finite; a program needn't handle non-finite values.
Results may differ from a plain program's by a relative error of at most 0.012.
Values may be sent and summed in bfloat16 or wider, within the bound.
A program may use at most 128 MiB of HBM per device.

v0:
```python
import jax
import jax.numpy as jnp
from jax import lax
from jax.sharding import PartitionSpec as P


def rms_scale(values, gain):
    wide = values.astype(jnp.float32)
    mean_sq = jnp.mean(wide * wide, axis=-1, keepdims=True)
    return (wide * lax.rsqrt(mean_sq + 1e-06) * gain).astype(jnp.bfloat16)


def expert_part(rows, gate_up_w, down_w):
    quarter = down_w.shape[1]
    gate_up = jnp.dot(rows, gate_up_w, preferred_element_type=jnp.float32)
    act = (jax.nn.silu(gate_up[:, :quarter]) * gate_up[:, quarter:]).astype(jnp.bfloat16)
    return lax.dot_general(
        act, down_w, (((1,), (1,)), ((), ())), preferred_element_type=jnp.float32
    )


def on_device(
    hidden,
    norm_gain,
    expert_in,
    expert_out,
    expert_ids,
    gate_levels,
    shared_gate,
    shared_up,
    shared_down,
    next_gain,
    kv_weight,
):
    tok_rows, width = hidden.shape
    top = expert_ids.shape[1]
    n_mp = lax.axis_size("mp")
    n_groups = lax.axis_size(("dp", "expert"))
    capacity = min(tok_rows, (2 * tok_rows * top + n_groups - 1) // n_groups)
    local_e, local_rows, double = expert_in.shape
    full_ff = double // 2
    quarter = full_ff // n_mp
    in_cast = (
        expert_in.astype(jnp.bfloat16)
        .reshape(local_e, local_rows, 2, n_mp, quarter)
        .transpose(0, 3, 1, 2, 4)
    )
    out_cast = (
        expert_out.astype(jnp.bfloat16)
        .reshape(local_e, local_rows, n_mp, quarter)
        .transpose(0, 2, 1, 3)
    )
    in_send = in_cast.reshape(local_e * n_mp, local_rows, 2, quarter)
    out_send = out_cast.reshape(local_e * n_mp, local_rows, quarter)
    in_recv, out_recv = (
        lax.all_to_all(in_send, ("expert", "mp"), split_axis=0, concat_axis=1, tiled=True),
        lax.all_to_all(out_send, ("expert", "mp"), split_axis=0, concat_axis=1, tiled=True),
    )
    gate_up_w = in_recv.reshape(width, 2 * quarter)
    down_w = out_recv.reshape(width, quarter)
    normed = rms_scale(hidden, norm_gain)
    levels = gate_levels.astype(jnp.float32)
    gate_weights = levels / jnp.sum(levels, axis=1, keepdims=True)
    flat_ids = expert_ids.reshape(-1)
    pairs = flat_ids.shape[0]
    onehot = (flat_ids[:, None] == jnp.arange(n_groups, dtype=jnp.int32)[None, :]).astype(jnp.int32)
    before = jnp.cumsum(onehot, axis=0) - onehot
    slot_of_pair = jnp.sum(before * onehot, axis=1)
    target = flat_ids * capacity + slot_of_pair
    token_of_pair = jnp.arange(pairs, dtype=jnp.int32) // top
    send = (
        jnp.zeros((n_groups * capacity, width), jnp.bfloat16).at[target].set(normed[token_of_pair])
    )
    received = lax.all_to_all(
        send.reshape(n_groups, capacity, width),
        ("dp", "expert"),
        split_axis=0,
        concat_axis=0,
        tiled=True,
    )
    slots_here = received.reshape(n_groups * capacity, width)
    every_slot = lax.all_gather(slots_here, "mp", axis=0, tiled=True)
    rows = every_slot
    summed = lax.psum_scatter(
        expert_part(rows, gate_up_w, down_w).astype(jnp.bfloat16),
        "mp",
        scatter_dimension=0,
        tiled=True,
    )
    result = summed.reshape(n_groups, capacity, width)
    back = lax.all_to_all(
        result, ("dp", "expert"), split_axis=0, concat_axis=0, tiled=True
    ).reshape(n_groups * capacity, width)
    picked = back[target].reshape(tok_rows, top, width)
    routed = jnp.sum(picked.astype(jnp.float32) * gate_weights[:, :, None], axis=1)
    gate_w, up_w, down_s = (
        lax.all_gather(shared_gate, ("dp", "expert"), axis=0, tiled=True),
        lax.all_gather(shared_up, ("dp", "expert"), axis=0, tiled=True),
        lax.all_gather(shared_down, ("dp", "expert"), axis=0, tiled=True),
    )
    group_rows = lax.all_gather(normed, "mp", axis=0, tiled=True)
    rows = group_rows
    gate_part = jnp.dot(rows, gate_w, preferred_element_type=jnp.float32)
    up_part = jnp.dot(rows, up_w, preferred_element_type=jnp.float32)
    act = (jax.nn.silu(gate_part) * up_part).astype(jnp.bfloat16)
    shared_out = lax.psum_scatter(
        lax.dot_general(act, down_s, (((1,), (1,)), ((), ())), preferred_element_type=jnp.float32),
        "mp",
        scatter_dimension=0,
        tiled=True,
    )
    layer_out = (hidden.astype(jnp.float32) + routed + shared_out).astype(jnp.bfloat16)
    next_rows = rms_scale(layer_out, next_gain)
    next_group = lax.all_gather(next_rows, "mp", axis=0, tiled=True)
    kv_latent = jnp.dot(next_group, kv_weight, preferred_element_type=jnp.float32).astype(
        jnp.bfloat16
    )
    return (layer_out, kv_latent)


def solution(mesh):
    in_specs = (
        P(("dp", "expert", "mp"), None),
        P(),
        P("dp", ("expert", "mp"), None),
        P("dp", ("expert", "mp"), None),
        P(("dp", "expert", "mp"), None),
        P(("dp", "expert", "mp"), None),
        P(("dp", "expert"), "mp"),
        P(("dp", "expert"), "mp"),
        P(("dp", "expert"), "mp"),
        P(),
        P(None, "mp"),
    )
    out_specs = (P(("dp", "expert", "mp"), None), P(("dp", "expert"), "mp"))
    return jax.shard_map(
        on_device, mesh=mesh, in_specs=in_specs, out_specs=out_specs, check_vma=False
    )
```

profile of v0, /device:TPU:8, one launch (start us, length us, event | category | flops | bytes accessed | tf_op | source)
XLA Modules:
  0.0 569.9 jit_solution(8128432649492718918)
XLA Ops:
  8.0 0.9 copy.31
  8.9 0.1 eq.29
  9.0 0.1 eq.25
  9.2 0.7 broadcast_multiply_fusion
  9.9 0.9 reduce-window.6
  10.8 0.2 slice_reduce_fusion
  11.0 0.1 copy.30
  11.1 0.1 mul.81
  11.3 1.1 fusion.11
  12.5 1.1 fusion.13
  13.6 10.0 %scatter_custom_fusion = bf16[768,2048]{1,0:T(8,128)(2,1)} fusion(s32[384]{0:T(512)S(1)} %fusion.21, bf16[64,2048]{1,0:T(8,128)(2,1)S(1)} %fusion.13, s32[1024]{0:T(1024)S(1)} %pad_clamp_fusion.1, bf16[]{:T(256)} %constant.12.clone.1), kind=kCustom, calls=%fused_computation.11 | custom fusion | bytes 3145730 | tf_op jit(solution)/shard_map/scatter | solution.py:72
  23.6 6.3 %all-to-all-start = ((bf16[16,48,2048]{2,1,0:T(8,128)(2,1)}), bf16[16,48,2048]{2,1,0:T(8,128)(2,1)}, u32[]{:S(2)}, u32[]{:S(2)}) async-start(bf16[16,48,2048]{2,1,0:T(8,128)(2,1)} %bitcast.49), calls=%async_computation | async-start | bytes 6291456 | tf_op jit(solution)/shard_map/all_to_all | solution.py:74
  29.9 2.9 convert_element_type.56
  32.8 0.8 fusion.26
  33.6 2.0 pad_maximum_fusion
  35.6 4.6 copy.38
  40.2 58.0 %all-to-all-done = bf16[16,48,2048]{2,1,0:T(8,128)(2,1)} async-done(((bf16[16,48,2048]{2,1,0:T(8,128)(2,1)}), bf16[16,48,2048]{2,1,0:T(8,128)(2,1)}, u32[]{:S(2)}, u32[]{:S(2)}) %all-to-all-start) | async-done | bytes 3145760 | tf_op jit(solution)/shard_map/all_to_all | solution.py:74
  98.2 5.2 all-to-all-start.2
  103.4 0.7 all-gather.5.cloned.1.call-update
  104.1 9.6 %copy.34 = bf16[4,256,2816]{1,2,0:T(8,128)(2,1)} copy(f32[4,256,2816]{2,1,0:T(8,128)} %param.13) | data formatting | bytes 17301504 | tf_op args[2]
  113.7 6.5 %copy.35 = bf16[4,2,256,2,704]{2,4,3,1,0:T(8,128)(2,1)} copy(bf16[4,2,256,2,704]{2,4,1,3,0:T(8,128)(2,1)} %bitcast.48) | data formatting | bytes 11534336 | tf_op jit(solution)/shard_map/transpose | solution.py:46
  120.3 35.6 %all-to-all-done.2 = bf16[8,256,704]{1,2,0:T(8,128)(2,1)} async-done(((bf16[8,256,704]{1,2,0:T(8,128)(2,1)}), bf16[8,256,704]{1,2,0:T(8,128)(2,1)}, u32[]{:S(2)}, u32[]{:S(2)}) %all-to-all-start.2) | async-done | bytes 2883616 | tf_op jit(solution)/shard_map/all_to_all | solution.py:57
  155.9 4.7 all-to-all-start.1
  160.6 3.8 copy.44
  164.5 103.4 %all-to-all-done.1 = bf16[8,256,2,704]{1,3,2,0:T(8,128)(2,1)} async-done(((bf16[8,256,2,704]{1,3,2,0:T(8,128)(2,1)}), bf16[8,256,2,704]{1,3,2,0:T(8,128)(2,1)}, u32[]{:S(2)}, u32[]{:S(2)}) %all-to-all-start.1) | async-done | bytes 5767200 | tf_op jit(solution)/shard_map/all_to_all | solution.py:56
  267.8 5.9 %copy.36 = bf16[8,256,2,704]{1,0,3,2:T(8,128)(2,1)S(1)} copy(bf16[8,256,2,704]{1,3,2,0:T(8,128)(2,1)} %all-to-all-done.1) | data formatting | bytes 11534336 | tf_op jit(solution)/shard_map/all_to_all | solution.py:56
  273.8 5.0 copy.45
  278.8 13.4 %fusion.27 = f32[1536,1408]{0,1:T(8,128)S(1)} fusion(bf16[1536,2048]{1,0:T(8,128)(2,1)} %all-gather.5.cloned.1.call-done, bf16[2048,1408]{0,1:T(8,128)(2,1)} %bitcast.51), kind=kOutput, calls=%fused_computation.57 | convolution fusion | flops 8858370048 | bytes 20709376 | tf_op jit(solution)/shard_map/dot_general | solution.py:15
  292.2 7.3 %convolution_convert_fusion = bf16[1536,2048]{1,0:T(8,128)(2,1)} fusion(bf16[2048,704]{0,1:T(8,128)(2,1)S(1)} %bitcast.53, f32[1536,1408]{0,1:T(8,128)S(1)} %fusion.27), kind=kOutput, calls=%fused_computation.3 | convolution fusion | flops 4438818816 | bytes 17825792 | tf_op jit(solution)/shard_map/dot_general | solution.py:17
  299.6 0.5 all-gather.7.cloned.1.call-update
  300.2 0.5 all-gather.11.cloned.1.call-update
  300.8 0.5 all-gather.9.cloned.1.call-update
  301.3 74.5 %reduce-scatter.3.cloned.1.call-done = bf16[768,2048]{1,0:T(8,128)(2,1)} async-done(((bf16[1536,2048]{1,0:T(8,128)(2,1)}), bf16[768,2048]{1,0:T(8,128)(2,1)}) %reduce-scatter.3.cloned.1.call-update) | async-done | bytes 3145744 | tf_op jit(solution)/shard_map/reduce_scatter | solution.py:84
  375.8 6.1 %all-to-all-start.3 = ((bf16[16,48,2048]{2,1,0:T(8,128)(2,1)}), bf16[16,48,2048]{2,1,0:T(8,128)(2,1)}, u32[]{:S(2)}, u32[]{:S(2)}) async-start(bf16[16,48,2048]{2,1,0:T(8,128)(2,1)} %bitcast.52), calls=%async_computation.4 | async-start | bytes 6291456 | tf_op jit(solution)/shard_map/all_to_all | solution.py:91
  381.9 9.0 %all_gather.19 = bf16[128,2048]{1,0:T(8,128)(2,1)S(1)} all-gather(bf16[64,2048]{1,0:T(8,128)(2,1)S(1)} %fusion.13), channel_id=1, replica_groups=mesh['dp'=4,'expert'=4,'mp'=2] {'mp'}, dimensions={0}, use_global_device_ids=true | all-gather | bytes 786432 | tf_op jit(solution)/shard_map/all_gather | solution.py:101
  391.0 3.6 fusion.28
  394.6 65.7 %all-gather.11.cloned.1.call-done = bf16[2048,1408]{1,0:T(8,128)(2,1)} async-done(((bf16[128,1408]{1,0:T(8,128)(2,1)}), bf16[2048,1408]{1,0:T(8,128)(2,1)}) %all-gather.11.cloned.1.call-update) | async-done | bytes 5767184 | tf_op jit(solution)/shard_map/all_gather | solution.py:99
  460.3 63.8 %all-gather.9.cloned.1.call-done = bf16[2048,1408]{1,0:T(8,128)(2,1)} async-done(((bf16[128,1408]{1,0:T(8,128)(2,1)}), bf16[2048,1408]{1,0:T(8,128)(2,1)}) %all-gather.9.cloned.1.call-update) | async-done | bytes 5767184 | tf_op jit(solution)/shard_map/all_gather | solution.py:98
  524.0 8.2 %fusion.7 = f32[128,2048]{1,0:T(8,128)} fusion(bf16[2048,1408]{1,0:T(8,128)(2,1)} %all-gather.11.cloned.1.call-done, bf16[128,2048]{1,0:T(8,128)(2,1)S(1)} %all_gather.19, bf16[2048,1408]{1,0:T(8,128)(2,1)} %all-gather.9.cloned.1.call-done, f32[128,1408]{1,0:T(8,128)S(1)} %fusion.28), kind=kOutput, calls=%fused_computation.18 | convolution fusion | flops 1477476352 | bytes 13828096 | tf_op jit(solution)/shard_map/dot_general | solution.py:107
  532.3 0.1 copy.40
  532.4 6.9 %gather_fusion = bf16[384,2048]{1,0:T(8,128)(2,1)S(1)} fusion(bf16[768,2048]{1,0:T(8,128)(2,1)} %bitcast.8, s32[1024]{0:T(1024)S(1)} %pad_clamp_fusion), kind=kCustom, calls=%fused_computation.1 | custom fusion | bytes 3147264 | tf_op jit(solution)/shard_map/gather | solution.py:94
  539.4 2.1 reshape.162
  541.5 3.8 multiply_reduce_fusion
  545.3 6.0 %reduce-scatter.5.cloned.1.call-done = f32[64,2048]{1,0:T(8,128)} async-done(((f32[128,2048]{1,0:T(8,128)}), f32[64,2048]{1,0:T(8,128)}) %reduce-scatter.5.cloned.1.call-update) | async-done | bytes 524304 | tf_op jit(solution)/shard_map/reduce_scatter | solution.py:106
  551.3 1.2 fusion.8
  552.6 0.1 fusion.10
  552.7 8.7 %all_gather.23 = bf16[128,2048]{1,0:T(8,128)(2,1)S(1)} all-gather(bf16[64,2048]{1,0:T(8,128)(2,1)S(1)} %fusion.10), channel_id=1, replica_groups=mesh['dp'=4,'expert'=4,'mp'=2] {'mp'}, dimensions={0}, use_global_device_ids=true | all-gather | bytes 786432 | tf_op jit(solution)/shard_map/all_gather | solution.py:114
  561.5 1.1 convolution_convert_fusion.1
  (34 shorter events, 0.6 us)
Async XLA Ops:
  8.0 553.5 %copy-start = (bf16[2048,288]{0,1:T(8,128)(2,1)S(1)}, bf16[2048,288]{0,1:T(8,128)(2,1)}, u32[]{:S(2)}) copy-start(bf16[2048,288]{0,1:T(8,128)(2,1)} %param.21) | copy-start | bytes 3538948
  23.6 74.6 %all-to-all-start = ((bf16[16,48,2048]{2,1,0:T(8,128)(2,1)}), bf16[16,48,2048]{2,1,0:T(8,128)(2,1)}, u32[]{:S(2)}, u32[]{:S(2)}) async-start(bf16[16,48,2048]{2,1,0:T(8,128)(2,1)} %bitcast.49), calls=%async_computation | async-start | bytes 6291456 | tf_op jit(solution)/shard_map/all_to_all | solution.py:74
  98.2 57.6 %all-to-all-start.2 = ((bf16[8,256,704]{1,2,0:T(8,128)(2,1)}), bf16[8,256,704]{1,2,0:T(8,128)(2,1)}, u32[]{:S(2)}, u32[]{:S(2)}) async-start(bf16[8,256,704]{1,2,0:T(8,128)(2,1)} %copy.38), calls=%async_computation.2 | async-start | bytes 5767168 | tf_op jit(solution)/shard_map/all_to_all | solution.py:57
  103.4 175.4 %all-gather.5.cloned.1.call-start = ((), (), s32[]{:S(2)}) async-start(), calls=%async_computation.6 | async-start | bytes 9437184 | tf_op jit(solution)/shard_map/all_gather | solution.py:82
  155.9 112.0 %all-to-all-start.1 = ((bf16[8,256,2,704]{1,3,2,0:T(8,128)(2,1)}), bf16[8,256,2,704]{1,3,2,0:T(8,128)(2,1)}, u32[]{:S(2)}, u32[]{:S(2)}) async-start(bf16[8,256,2,704]{1,3,2,0:T(8,128)(2,1)} %bitcast.46), calls=%async_computation.1 | async-start | bytes 11534336 | tf_op jit(solution)/shard_map/all_to_all | solution.py:56
  160.6 215.2 %reduce-scatter.3.cloned.1.call-start = ((), (), s32[]{:S(2)}) async-start(), calls=%async_computation.7 | async-start | bytes 9437184 | tf_op jit(solution)/shard_map/reduce_scatter | solution.py:84
  278.8 13.4 %copy-start.1 = (bf16[8,88,8,256]{3,2,0,1:T(8,128)(2,1)S(1)}, bf16[8,88,8,256]{3,2,0,1:T(8,128)(2,1)}, u32[]{:S(2)}) copy-start(bf16[8,88,8,256]{3,2,0,1:T(8,128)(2,1)} %copy.44) | copy-start | bytes 8650756
  299.5 91.4 %all-gather.7.cloned.1.call-start = ((), (), s32[]{:S(2)}) async-start(), calls=%async_computation.8 | async-start | bytes 6127616 | tf_op jit(solution)/shard_map/all_gather | solution.py:97
  300.1 160.2 %all-gather.11.cloned.1.call-start = ((), (), s32[]{:S(2)}) async-start(), calls=%async_computation.10 | async-start | bytes 6127616 | tf_op jit(solution)/shard_map/all_gather | solution.py:99
  300.7 223.3 %all-gather.9.cloned.1.call-start = ((), (), s32[]{:S(2)}) async-start(), calls=%async_computation.9 | async-start | bytes 6127616 | tf_op jit(solution)/shard_map/all_gather | solution.py:98
  375.8 156.6 %all-to-all-start.3 = ((bf16[16,48,2048]{2,1,0:T(8,128)(2,1)}), bf16[16,48,2048]{2,1,0:T(8,128)(2,1)}, u32[]{:S(2)}, u32[]{:S(2)}) async-start(bf16[16,48,2048]{2,1,0:T(8,128)(2,1)} %bitcast.52), calls=%async_computation.4 | async-start | bytes 6291456 | tf_op jit(solution)/shard_map/all_to_all | solution.py:91
  381.9 169.5 %reduce-scatter.5.cloned.1.call-start = ((), (), s32[]{:S(2)}) async-start(), calls=%async_computation.11 | async-start | bytes 1572864 | tf_op jit(solution)/shard_map/reduce_scatter | solution.py:106
  394.6 137.7 %copy-start.4 = (s32[64,6]{0,1:T(8,128)S(1)}, s32[64,6]{0,1:T(8,128)}, u32[]{:S(2)}) copy-start(s32[64,6]{0,1:T(8,128)} %param.16) | copy-start | bytes 4612
  539.4 12.0 %copy-start.2 = (bf16[64,2048]{1,0:T(8,128)(2,1)S(1)}, bf16[64,2048]{1,0:T(8,128)(2,1)}, u32[]{:S(2)}) copy-start(bf16[64,2048]{1,0:T(8,128)(2,1)} %param.11) | copy-start | bytes 786436
  541.5 11.1 %copy-start.5 = (f32[2048]{0:T(1024)S(1)}, f32[2048]{0:T(1024)}, u32[]{:S(2)}) copy-start(f32[2048]{0:T(1024)} %param.20) | copy-start | bytes 24580
  552.6 10.0 %copy-start.3 = (bf16[64,2048]{1,0:T(8,128)(2,1)}, bf16[64,2048]{1,0:T(8,128)(2,1)S(1)}, u32[]{:S(2)}) copy-start(bf16[64,2048]{1,0:T(8,128)(2,1)S(1)} %get-tuple-element.3) | copy-start | bytes 786436
Sparse Core Ops, SparseCore 0:
  105.8 140.5 all-gather.4
  299.7 76.0 reduce-scatter.2
  532.4 18.9 reduce-scatter.4
Sparse Core Ops, SparseCore 1:
  302.6 57.8 all-gather.6
  362.9 97.4 all-gather.10
  462.7 61.3 all-gather.8
where the time goes:
time: 573 us; the launch traced here: 570 us
  waiting for transfers between devices  409 us (71%)
  local copies, waits for them, and re-layouts  57.1 us (10%)
  matrix products  33.6 us (6%)
  starting transfers between devices  22.5 us (4%)
  blocking collectives  17.8 us (3%)
  between operations  15.6 us (3%)
  other arithmetic  14.1 us (2%)
    all_to_all x1, waiting for transfers between devices, on_device(): lax.all_to_all(in_send, ('expert', 'mp'), split_axis=0, concat_axis=1, ti...  103 us
    reduce_scatter x1, waiting for transfers between devices, on_device(): lax.psum_scatter(expert_part(rows, gate_up_w, down_w).astype(jnp.bfloat16...  74.5 us
    all_gather x1, waiting for transfers between devices, on_device(): lax.all_gather(shared_down, ('dp', 'expert'), axis=0, tiled=True)  65.7 us
    all_gather x1, waiting for transfers between devices, on_device(): lax.all_gather(shared_up, ('dp', 'expert'), axis=0, tiled=True)  63.8 us
    all_to_all x1, waiting for transfers between devices, on_device(): lax.all_to_all(send.reshape(n_groups, capacity, width), ('dp', 'expert'),...  58 us
    all_to_all x1, waiting for transfers between devices, on_device(): lax.all_to_all(out_send, ('expert', 'mp'), split_axis=0, concat_axis=1, t...  35.6 us
    unnamed x15, local copies, waits for them, and re-layouts  15.5 us
    dot_general x1, matrix products, expert_part(): gate_up = jnp.dot(rows, gate_up_w, preferred_element_type=jnp.float32)  13.4 us
  transfers between devices with their start and end apart: 10, of which 7 were waited for; matrix products, arithmetic and copies ran while one was open for 12% of the time, Pallas kernels for 0%

commit v1 on v0

--- a/solution.py
+++ b/solution.py
@@ -1,7 +1,457 @@
+import functools
+
 import jax
 import jax.numpy as jnp
 from jax import lax
+from jax.experimental import pallas as pl
+from jax.experimental.pallas import tpu as pltpu
 from jax.sharding import PartitionSpec as P
+
+MESH = pl.DeviceIdType.MESH
+LANES = 128
+VMEM_BYTES = 56 * 1024 * 1024
+
+
+def position():
+    return lax.axis_index("dp"), lax.axis_index("expert"), lax.axis_index("mp")
+
+
+def barrier(peers):
+    sem = pltpu.get_barrier_semaphore()
+    for peer in peers:
+        pl.semaphore_signal(sem, inc=1, device_id=peer, device_id_type=MESH)
+    pl.semaphore_wait(sem, len(peers))
+
+
+def pack_kernel(in_ref, out_ref, in_pack, out_pack):
+    rows, full = out_ref.shape[1:]
+    main = full // (2 * LANES) * LANES
+    mid = main + LANES
+    half = LANES // 2
+    low = lax.broadcasted_iota(jnp.int32, (rows, LANES), 1) < half
+    for first, core in ((0, 0), (mid, 1)):
+        in_pack[core, :, :main] = in_ref[0, :, first : first + main].astype(jnp.bfloat16)
+        in_pack[core, :, main : 2 * main] = in_ref[
+            0, :, full + first : full + first + main
+        ].astype(jnp.bfloat16)
+        out_pack[core, :, :main] = out_ref[0, :, first : first + main].astype(jnp.bfloat16)
+    gate = in_ref[0, :, main:mid]
+    up = in_ref[0, :, full + main : full + mid]
+    down = out_ref[0, :, main:mid]
+    in_pack[0, :, 2 * main :] = jnp.where(low, gate, pltpu.roll(up, half, 1)).astype(jnp.bfloat16)
+    in_pack[1, :, 2 * main :] = jnp.where(low, pltpu.roll(gate, half, 1), up).astype(jnp.bfloat16)
+    out_pack[0, :, main:] = jnp.where(low, down, 0.0).astype(jnp.bfloat16)
+    out_pack[1, :, main:] = jnp.where(low, pltpu.roll(down, half, 1), 0.0).astype(jnp.bfloat16)
+
+
+def pack(expert_in, expert_out):
+    local_e, rows, double = expert_in.shape
+    full = double // 2
+    wide = (full // (2 * LANES) + 1) * LANES
+    tile = 128
+    return pl.pallas_call(
+        pack_kernel,
+        grid=(local_e, rows // tile),
+        in_specs=[
+            pl.BlockSpec((1, tile, double), lambda e, i: (e, i, 0)),
+            pl.BlockSpec((1, tile, full), lambda e, i: (e, i, 0)),
+        ],
+        out_specs=[
+            pl.BlockSpec((2, tile, full), lambda e, i: (e, i, 0)),
+            pl.BlockSpec((2, tile, wide), lambda e, i: (e, i, 0)),
+        ],
+        out_shape=[
+            jax.ShapeDtypeStruct((2 * local_e, rows, full), jnp.bfloat16),
+            jax.ShapeDtypeStruct((2 * local_e, rows, wide), jnp.bfloat16),
+        ],
+        compiler_params=pltpu.CompilerParams(vmem_limit_bytes=VMEM_BYTES),
+    )(expert_in, expert_out)
+
+
+def gather_kernel(
+    n_dp, n_exp, tok, w_in, w_out, s_in, s_out, all_tok, gu, dn,
+    z_s, z_r, h_s, h_r, f_s, f_r, win_s, win_r, wout_s, wout_r, sin_s, sin_r, sout_s, sout_r, local,
+):
+    dp, ex, mp = position()
+    block = tok.shape[0]
+    in_cols, out_cols = w_in.shape[2], w_out.shape[2]
+    w_rows, s_rows = w_in.shape[1], s_in.shape[1]
+    mate = (dp, ex + 1 - 2 * lax.rem(ex, 2), mp)
+    xpeer = (dp, ex, 1 - mp)
+    ypeer = (dp, lax.rem(ex + n_exp // 2, n_exp), mp)
+    plane = [
+        (a, b) for a in range(n_exp) for b in range(2) if (a, b) != (0, 0)
+    ]
+    column = [
+        (a, b) for a in range(n_dp) for b in range(n_exp) if (a, b) != (0, 0)
+    ]
+
+    def in_plane(a, b):
+        return (dp, lax.rem(ex + a, n_exp), lax.rem(mp + b, 2))
+
+    def in_column(a, b):
+        return (lax.rem(dp + a, n_dp), lax.rem(ex + b, n_exp), mp)
+
+    barrier(
+        [in_plane(a, b) for a, b in plane] + [in_column(a, b) for a, b in column if a != 0]
+    )
+
+    def rows_of(k, e, m):
+        index = (lax.rem(dp + n_dp - k, n_dp) * n_exp + e) * 2 + m
+        return pl.ds(pl.multiple_of(index * block, block), block)
+
+    started = []
+
+    def send(src, dst, s, r, to):
+        copy = pltpu.make_async_remote_copy(
+            src_ref=src, dst_ref=dst, send_sem=s, recv_sem=r, device_id=to, device_id_type=MESH
+        )
+        copy.start()
+        started.append(copy)
+        return copy
+
+    mine = rows_of(0, ex, mp)
+    from_z = {}
+    for k in range(1, n_dp):
+        from_z[k] = send(
+            tok, all_tok.at[mine], z_s.at[k], z_r.at[k], (lax.rem(dp + k, n_dp), ex, mp)
+        )
+    own = pltpu.make_async_copy(tok, all_tok.at[mine], local.at[0])
+    own.start()
+    from_h = {}
+
+    def spread(k, src):
+        rows = rows_of(k, ex, mp)
+        for way, to in enumerate((xpeer, ypeer, mate)):
+            at = way * n_dp + k
+            from_h[way, k] = send(src, all_tok.at[rows], h_s.at[at], h_r.at[at], to)
+
+    spread(0, tok)
+
+    w_at = pl.ds(pl.multiple_of((ex * 2 + mp) * w_rows, w_rows), w_rows)
+    s_at = pl.ds(pl.multiple_of((dp * n_exp + ex) * s_rows, s_rows), s_rows)
+    rest = []
+    locals_ = [own]
+    pieces = (
+        (w_in, gu.at[w_at, pl.ds(0, in_cols)], ex * 2 + mp),
+        (w_out, dn.at[w_at, pl.ds(0, out_cols)], ex * 2 + mp),
+        (s_in, gu.at[s_at, pl.ds(in_cols, s_in.shape[2])], dp * n_exp + ex),
+        (s_out, dn.at[s_at, pl.ds(out_cols, s_out.shape[2])], dp * n_exp + ex),
+    )
+    for at, (src, dst, index) in enumerate(pieces):
+        copy = pltpu.make_async_copy(src.at[index], dst, local.at[1 + at])
+        copy.start()
+        locals_.append(copy)
+    for at, (a, b) in enumerate(plane):
+        to = in_plane(a, b)
+        index = to[1] * 2 + to[2]
+        rest.append(send(w_in.at[index], pieces[0][1], win_s.at[at], win_r.at[at], to))
+        rest.append(send(w_out.at[index], pieces[1][1], wout_s.at[at], wout_r.at[at], to))
+    for at, (a, b) in enumerate(column):
+        to = in_column(a, b)
+        index = to[0] * n_exp + to[1]
+        rest.append(send(s_in.at[index], pieces[2][1], sin_s.at[at], sin_r.at[at], to))
+        rest.append(send(s_out.at[index], pieces[3][1], sout_s.at[at], sout_r.at[at], to))
+
+    for k in range(1, n_dp):
+        from_z[k].wait_recv()
+        spread(k, all_tok.at[rows_of(k, ex, mp)])
+    from_f = {}
+
+    def forward(kind, k, rows, to):
+        at = kind * n_dp + k
+        from_f[kind, k] = send(all_tok.at[rows], all_tok.at[rows], f_s.at[at], f_r.at[at], to)
+
+    y_ex = ypeer[1]
+    for k in range(n_dp):
+        from_h[0, k].wait_recv()
+        rows = rows_of(k, ex, 1 - mp)
+        if k < n_dp // 2:
+            forward(0, k, rows, ypeer)
+        forward(1, k, rows, mate)
+        from_h[1, k].wait_recv()
+        rows = rows_of(k, y_ex, mp)
+        if k >= n_dp // 2:
+            forward(0, k, rows, xpeer)
+        forward(2, k, rows, mate)
+    for k in range(n_dp):
+        from_f[0, k].wait_recv()
+        forward(3, k, rows_of(k, y_ex, 1 - mp), mate)
+    for k in range(n_dp):
+        from_h[2, k].wait_recv()
+        for kind in (1, 2, 3):
+            from_f[kind, k].wait_recv()
+    for copy in rest:
+        copy.wait_recv()
+    for copy in started:
+        copy.wait_send()
+    for copy in locals_:
+        copy.wait()
+
+
+def gather(n_dp, n_exp, tok, w_in, w_out, s_in, s_out):
+    total = tok.shape[0] * n_dp * n_exp * 2
+    depth = w_in.shape[1] * n_exp * 2
+    n_plane, n_column = n_exp * 2 - 1, n_dp * n_exp - 1
+    counts = [n_dp] * 2 + [3 * n_dp] * 2 + [4 * n_dp] * 2
+    counts += [n_plane] * 4 + [n_column] * 4 + [5]
+    return pl.pallas_call(
+        functools.partial(gather_kernel, n_dp, n_exp),
+        in_specs=[pl.BlockSpec(memory_space=pl.ANY)] * 5,
+        out_specs=[pl.BlockSpec(memory_space=pl.ANY)] * 3,
+        out_shape=[
+            jax.ShapeDtypeStruct((total, tok.shape[1]), jnp.bfloat16),
+            jax.ShapeDtypeStruct((depth, w_in.shape[2] + s_in.shape[2]), jnp.bfloat16),
+            jax.ShapeDtypeStruct((depth, w_out.shape[2] + s_out.shape[2]), jnp.bfloat16),
+        ],
+        scratch_shapes=[pltpu.SemaphoreType.DMA((count,)) for count in counts],
+        compiler_params=pltpu.CompilerParams(
+            collective_id=0, has_side_effects=True, vmem_limit_bytes=VMEM_BYTES
+        ),
+    )(tok, w_in, w_out, s_in, s_out)
+
+
+def silu(v):
+    return v / (1.0 + jnp.exp(-v))
+
+
+def expert_kernel(n_exp, experts, in_cols, out_cols, tok_ref, gu_ref, dn_ref, part_ref):
+    dp, ex, _ = position()
+    width = gu_ref.shape[0]
+    mine = dp * n_exp + ex
+    rows = tok_ref.shape[0]
+    lane = lax.broadcasted_iota(jnp.int32, (rows, LANES), 1)
+    extra = tok_ref[:, width:].astype(jnp.float32)
+    weight = jnp.sum(
+        jnp.where((lane == mine) | (lane == mine + experts), extra, 0.0), axis=1, keepdims=True
+    )
+    hid = jnp.dot(tok_ref[:, :width], gu_ref[...], preferred_element_type=jnp.float32)
+    main = out_cols - LANES
+    act = silu(hid[:, :main]) * hid[:, main : 2 * main] * weight
+    mixed = hid[:, 2 * main : in_cols]
+    mixed_act = silu(mixed) * pltpu.roll(mixed, LANES // 2, 1) * weight
+    mixed_act = jnp.where(lane < LANES // 2, mixed_act, 0.0)
+    span = (hid.shape[1] - in_cols) // 2
+    shared = silu(hid[:, in_cols : in_cols + span]) * hid[:, in_cols + span :]
+    acts = jnp.concatenate([act, mixed_act, shared], axis=1).astype(jnp.bfloat16)
+    part_ref[...] = lax.dot_general(
+        acts, dn_ref[...], (((1,), (1,)), ((), ())), preferred_element_type=jnp.float32
+    ).astype(jnp.bfloat16)
+
+
+def expert_dense(n_exp, experts, in_cols, out_cols, tok, gu, dn):
+    total, wide = tok.shape
+    width = gu.shape[0]
+    tile = 256
+    return pl.pallas_call(
+        functools.partial(expert_kernel, n_exp, experts, in_cols, out_cols),
+        grid=(total // tile,),
+        in_specs=[
+            pl.BlockSpec((tile, wide), lambda i: (i, 0)),
+            pl.BlockSpec(gu.shape, lambda i: (0, 0)),
+            pl.BlockSpec(dn.shape, lambda i: (0, 0)),
+        ],
+        out_specs=pl.BlockSpec((tile, width), lambda i: (i, 0)),
+        out_shape=jax.ShapeDtypeStruct((total, width), jnp.bfloat16),
+        compiler_params=pltpu.CompilerParams(vmem_limit_bytes=VMEM_BYTES),
+    )(tok, gu, dn)
+
+
+def scale_rows(wide, gain):
+    mean_sq = jnp.mean(wide * wide, axis=-1, keepdims=True)
+    return (wide * lax.rsqrt(mean_sq + 1e-06) * gain).astype(jnp.bfloat16)
+
+
+def add(one, other):
+    return (one.astype(jnp.float32) + other.astype(jnp.float32)).astype(jnp.bfloat16)
+
+
+def reduce_kernel(
+    n_dp, n_exp, part, hidden, gain, kv_w, layer, kv,
+    r1, s1, r2x, r2y, s2, r3, s3, r4, rows_own, rows_peer,
+    c_s, c_r, x_s, x_r, y_s, y_r, b_s, b_r, z_s, z_r, k_s, k_r,
+):
+    dp, ex, mp = position()
+    block = hidden.shape[0]
+    y, core = ex // 2, lax.rem(ex, 2)
+    mate = (dp, ex + 1 - 2 * core, mp)
+    xpeer = (dp, ex, 1 - mp)
+    ypeer = (dp, lax.rem(ex + n_exp // 2, n_exp), mp)
+    zpeers = [(lax.rem(dp + k, n_dp), ex, mp) for k in range(1, n_dp)]
+    barrier([mate, xpeer, ypeer] + zpeers)
+    started = []
+
+    def send(src, dst, s, r, to):
+        copy = pltpu.make_async_remote_copy(
+            src_ref=src, dst_ref=dst, send_sem=s, recv_sem=r, device_id=to, device_id_type=MESH
+        )
+        copy.start()
+        started.append(copy)
+        return copy
+
+    half = n_dp // 2
+    order = [g for pair in zip(range(half), range(half, n_dp)) for g in pair]
+
+    def pair_rows(group, c):
+        index = (group // 2 * n_exp + group % 2 * 2 + c) * 2
+        return pl.ds(pl.multiple_of(index * block, 2 * block), 2 * block)
+
+    from_mate = {}
+    for d in order:
+        for g in (2 * d, 2 * d + 1):
+            from_mate[g] = send(
+                part.at[pair_rows(g, 1 - core)], r1.at[g], c_s.at[g], c_r.at[g], mate
+            )
+    mine = pl.ds(pl.multiple_of(mp * block, block), block)
+    theirs = pl.ds(pl.multiple_of((1 - mp) * block, block), block)
+    first_x, first_y = {}, {}
+    for d in order:
+        for g in (2 * d, 2 * d + 1):
+            from_mate[g].wait_recv()
+            s1[g] = add(part[pair_rows(g, core), :], r1[g])
+            if d < half:
+                first_x[g] = send(s1.at[g, theirs], r2x.at[g], x_s.at[g], x_r.at[g], xpeer)
+        if d >= half:
+            first_y[d] = send(
+                s1.at[2 * d + 1 - y], r2y.at[d - half], y_s.at[d - half], y_r.at[d - half], ypeer
+            )
+    second = {}
+    for d in order:
+        if d < half:
+            for j in range(2):
+                g = 2 * d + j
+                first_x[g].wait_recv()
+                s2[d, j] = add(s1[g, mine, :], r2x[g])
+            second[d] = send(s2.at[d, 1 - y], r3.at[d], b_s.at[d], b_r.at[d], ypeer)
+        else:
+            first_y[d].wait_recv()
+            both = add(s1[2 * d + y], r2y[d - half])
+            s2[d, 0] = both[:block]
+            s2[d, 1] = both[block:]
+            second[d] = send(s2.at[d, 1 - mp], r3.at[d], b_s.at[d], b_r.at[d], xpeer)
+    for d in order:
+        second[d].wait_recv()
+        s3[d] = add(s2[d, y if d < half else mp], r3[d])
+    third = []
+    for k in range(1, n_dp):
+        third.append(
+            send(
+                s3.at[lax.rem(dp + k, n_dp)], r4.at[k - 1], z_s.at[k - 1], z_r.at[k - 1],
+                zpeers[k - 1],
+            )
+        )
+    total = hidden[...].astype(jnp.float32) + s3[dp].astype(jnp.float32)
+    for k in range(1, n_dp):
+        third[k - 1].wait_recv()
+        total = total + r4[k - 1].astype(jnp.float32)
+    layer_rows = total.astype(jnp.bfloat16)
+    layer[...] = layer_rows
+    rows_own[...] = scale_rows(layer_rows.astype(jnp.float32), gain[...])
+    last = send(rows_own, rows_peer, k_s.at[0], k_r.at[0], xpeer)
+    kv[mine, :] = jnp.dot(
+        rows_own[...], kv_w[...], preferred_element_type=jnp.float32
+    ).astype(jnp.bfloat16)
+    last.wait_recv()
+    kv[theirs, :] = jnp.dot(
+        rows_peer[...], kv_w[...], preferred_element_type=jnp.float32
+    ).astype(jnp.bfloat16)
+    for copy in started:
+        copy.wait_send()
+
+
+def reduce_tail(n_dp, n_exp, part, hidden, gain, kv_w):
+    block, width = hidden.shape
+    half = n_dp // 2
+    bf16 = jnp.bfloat16
+    shapes = [
+        (2 * n_dp, 2 * block, width),
+        (2 * n_dp, 2 * block, width),
+        (2 * half, block, width),
+        (half, 2 * block, width),
+        (n_dp, 2, block, width),
+        (n_dp, block, width),
+        (n_dp, block, width),
+        (n_dp - 1, block, width),
+        (block, width),
+        (block, width),
+    ]
+    counts = [2 * n_dp] * 2 + [2 * half] * 2 + [half] * 2 + [n_dp] * 2 + [n_dp - 1] * 2 + [1] * 2
+    return pl.pallas_call(
+        functools.partial(reduce_kernel, n_dp, n_exp),
+        in_specs=[pl.BlockSpec(memory_space=pltpu.VMEM)] * 4,
+        out_specs=[pl.BlockSpec(memory_space=pltpu.VMEM)] * 2,
+        out_shape=[
+            jax.ShapeDtypeStruct((block, width), bf16),
+            jax.ShapeDtypeStruct((2 * block, kv_w.shape[1]), bf16),
+        ],
+        scratch_shapes=[pltpu.VMEM(shape, bf16) for shape in shapes]
+        + [pltpu.SemaphoreType.DMA((count,)) for count in counts],
+        compiler_params=pltpu.CompilerParams(
+            collective_id=1, has_side_effects=True, vmem_limit_bytes=VMEM_BYTES
+        ),
+    )(part, hidden, gain, kv_w)
+
+
+def pieces_of(weights, groups):
+    rows, columns = weights.shape
+    each = columns // groups
+    cut = weights.reshape(rows, groups, each).transpose(1, 0, 2)
+    return jnp.pad(cut, ((0, 0), (0, 0), (0, -each % LANES)))
+
+
+def dense_on_device(
+    hidden,
+    norm_gain,
+    expert_in,
+    expert_out,
+    expert_ids,
+    gate_levels,
+    shared_gate,
+    shared_up,
+    shared_down,
+    next_gain,
+    kv_weight,
+):
+    n_dp, n_exp = lax.axis_size("dp"), lax.axis_size("expert")
+    groups = n_dp * n_exp
+    experts = expert_in.shape[0] * n_dp
+    w_in, w_out = pack(expert_in, expert_out)
+    normed = scale_rows(hidden.astype(jnp.float32), norm_gain)
+    levels = gate_levels.astype(jnp.float32)
+    gate_weights = levels / jnp.sum(levels, axis=1, keepdims=True)
+    chosen = expert_ids[:, :, None] == jnp.arange(experts, dtype=jnp.int32)
+    spread = jnp.sum(jnp.where(chosen, gate_weights[:, :, None], 0.0), axis=1)
+    high = lax.reduce_precision(spread, 8, 7)
+    low = (spread - high).astype(jnp.bfloat16)
+    tok = jnp.concatenate(
+        [
+            normed,
+            high.astype(jnp.bfloat16),
+            low,
+            jnp.zeros((hidden.shape[0], LANES - 2 * experts), jnp.bfloat16),
+        ],
+        axis=1,
+    )
+    s_in = jnp.concatenate([pieces_of(shared_gate, groups), pieces_of(shared_up, groups)], axis=2)
+    s_out = pieces_of(shared_down, groups)
+    every, gu, dn = gather(n_dp, n_exp, tok, w_in, w_out, s_in, s_out)
+    part = expert_dense(n_exp, experts, w_in.shape[2], w_out.shape[2], every, gu, dn)
+    return tuple(reduce_tail(n_dp, n_exp, part, hidden, next_gain[None, :], kv_weight))
+
+
+def dense_fits(mesh, hidden, expert_in, expert_ids):
+    n_dp, n_exp, n_mp = (mesh.shape[name] for name in ("dp", "expert", "mp"))
+    tokens, width = hidden.shape
+    experts, _, double = expert_in.shape
+    return (
+        n_mp == 2
+        and n_exp == 4
+        and n_dp % 2 == 0
+        and experts == n_dp * n_exp
+        and 2 * experts <= LANES
+        and double // 2 % (2 * LANES) == LANES
+        and tokens * width <= 4 * 1024 * 1024
+    )
 
 
 def rms_scale(values, gain):
@@ -133,6 +583,15 @@
         P(None, "mp"),
     )
     out_specs = (P(("dp", "expert", "mp"), None), P(("dp", "expert"), "mp"))
-    return jax.shard_map(
-        on_device, mesh=mesh, in_specs=in_specs, out_specs=out_specs, check_vma=False
-    )
+
+    def run(*args):
+        dense = dense_fits(mesh, args[0], args[2], args[4])
+        return jax.shard_map(
+            dense_on_device if dense else on_device,
+            mesh=mesh,
+            in_specs=in_specs,
+            out_specs=out_specs,
+            check_vma=False,
+        )(*args)
+
+    return run

time: 573 us -> 294 us (0.51)
  waiting for transfers between devices: 409 us -> 0 us
  Pallas kernels: 0 us -> 279 us
  local copies, waits for them, and re-layouts: 57.1 us -> 8.37 us
  matrix products: 33.6 us -> 0 us
  starting transfers between devices: 22.5 us -> 0 us
  blocking collectives: 17.8 us -> 0 us
  between operations: 15.6 us -> 0.74 us
  other arithmetic: 14.1 us -> 5.52 us
    pallas_call x0 -> x4, Pallas kernels: none -> 279 us  [the longest x1 157 us: gather(): pl.pallas_call(functools.partial(gather_kernel, n_dp, n_exp), in_specs=[p...]
    all_to_all x4 -> x0, waiting for transfers between devices: 197 us -> none  [the longest x1 103 us: on_device(): lax.all_to_all(in_send, ('expert', 'mp'), split_axis=0, concat_axis=1, ti...]
    all_gather x4 -> x0, waiting for transfers between devices: 129 us -> none  [the longest x1 65.7 us: on_device(): lax.all_gather(shared_down, ('dp', 'expert'), axis=0, tiled=True)]
    reduce_scatter x2 -> x0, waiting for transfers between devices: 80.5 us -> none  [the longest x1 74.5 us: on_device(): lax.psum_scatter(expert_part(rows, gate_up_w, down_w).astype(jnp.bfloat16...]
    dot_general x5 -> x0, matrix products: 33.6 us -> none  [the longest x1 13.4 us: expert_part(): gate_up = jnp.dot(rows, gate_up_w, preferred_element_type=jnp.float32)]
    all_to_all x4 -> x0, starting transfers between devices: 22.3 us -> none  [the longest x1 6.3 us: on_device(): lax.all_to_all(send.reshape(n_groups, capacity, width), ('dp', 'expert'),...]
    all_gather x2 -> x0, blocking collectives: 17.8 us -> none  [the longest x1 9.04 us: on_device(): group_rows = lax.all_gather(normed, 'mp', axis=0, tiled=True)]
    unnamed x15 -> x13, local copies, waits for them, and re-layouts: 15.5 us -> 3.91 us
  transfers between devices with their start and end apart: 10 -> 0, of which waited for: 7 -> 0; matrix products, arithmetic and copies ran while one was open for 12% -> 0% of each run, Pallas kernels for 0% -> 0%
where the time goes in v1:
time: 294 us
  Pallas kernels  279 us (95%)
  local copies, waits for them, and re-layouts  8.37 us (3%)
  other arithmetic  5.52 us (2%)
    pallas_call x1, Pallas kernels, gather(): pl.pallas_call(functools.partial(gather_kernel, n_dp, n_exp), in_specs=[p...  157 us
    pallas_call x1, Pallas kernels, reduce_tail(): pl.pallas_call(functools.partial(reduce_kernel, n_dp, n_exp), in_specs=[p...  79.3 us
    pallas_call x1, Pallas kernels, expert_dense(): pl.pallas_call(functools.partial(expert_kernel, n_exp, experts, in_cols,...  30.9 us
    pallas_call x1, Pallas kernels, pack(): pl.pallas_call(pack_kernel, grid=(local_e, rows // tile), in_specs=[pl.Bl...  11.4 us

profile of v1, /device:TPU:8, one launch (start us, length us, event | category | flops | bytes accessed | tf_op | source)
XLA Modules:
  0.0 293.6 jit_solution(14340801568725524715)
XLA Ops:
  0.6 0.7 convert_reduce_fusion
  1.3 0.7 convert_divide_fusion
  2.0 0.7 select_reduce_fusion
  2.7 0.1 copy.37
  2.8 0.1 copy.38
  2.9 1.1 fusion.3
  4.0 1.1 fusion.5
  5.1 0.8 concatenate.6.tok
  6.0 0.0 copy-start.1
  6.0 0.0 copy-start.2
  6.0 11.4 %shard_map.122 = (bf16[8,256,1408]{2,1,0:T(8,128)(2,1)}, bf16[8,256,768]{2,1,0:T(8,128)(2,1)}) custom-call(f32[4,256,2816]{2,1,0:T(8,128)} %in_ref.1, f32[4,256,1408]{2,1,0:T(8,128)} %out_ref.1), custom_call_target="tpu_custom_call" | custom-call | tf_op jit(solution)/shard_map/pallas_call | solution.py:52
  17.4 0.0 copy-start.3
  17.4 0.0 copy-done.1
  17.4 0.2 copy.40
  17.6 0.3 copy.41
  17.9 0.0 copy-done.2
  17.9 0.2 copy.42
  18.1 0.3 copy.43
  18.4 1.2 fusion.2.s_in
  19.6 0.0 copy-done.3
  19.6 0.2 copy.44
  19.8 0.3 copy.45
  20.1 1.0 pad.12.s_out
  21.1 157.5 %shard_map.123 = (bf16[2048,2176]{1,0:T(8,128)(2,1)}, bf16[2048,1664]{1,0:T(8,128)(2,1)}, bf16[2048,896]{1,0:T(8,128)(2,1)}) custom-call(bf16[64,2176]{1,0:T(8,128)(2,1)} %concatenate.6.tok, bf16[8,256,1408]{2,1,0:T(8,128)(2,1)} %get-tuple-element.7.w_in, bf16[8,256,768]{2,1,0:T(8,128)(2,1)} %get-tuple-element.8.w_out, bf16[16,128,256]{2,1,0:T(8,128)(2,1)} %fusion.2.s_in, ...), custom_call_target="tpu_custom_call" | custom-call | tf_op jit(solution)/shard_map/pallas_call | solution.py:198
  178.6 0.0 copy-start
  178.6 30.9 %shard_map.124.part = bf16[2048,2048]{1,0:T(8,128)(2,1)} custom-call(bf16[2048,2176]{1,0:T(8,128)(2,1)} %get-tuple-element.9.tok_ref, bf16[2048,1664]{1,0:T(8,128)(2,1)} %get-tuple-element.10.gu_ref, bf16[2048,896]{1,0:T(8,128)(2,1)} %get-tuple-element.11.dn_ref), custom_call_target="tpu_custom_call" | custom-call | tf_op jit(solution)/shard_map/pallas_call | solution.py:246
  209.5 0.0 copy-done
  209.5 1.6 copy.46.kv_w
  211.0 79.3 %shard_map.125 = (bf16[64,2048]{1,0:T(8,128)(2,1)}, bf16[128,288]{1,0:T(8,128)(2,1)}) custom-call(bf16[2048,2048]{1,0:T(8,128)(2,1)} %shard_map.124.part, bf16[64,2048]{1,0:T(8,128)(2,1)} %hidden.1, f32[1,2048]{1,0:T(1,128)} %bitcast.13, bf16[2048,288]{1,0:T(8,128)(2,1)} %copy.46.kv_w), custom_call_target="tpu_custom_call" | custom-call | tf_op jit(solution)/shard_map/pallas_call | solution.py:379
  290.3 1.6 copy.47
  292.0 1.7 copy.49
  (4 shorter events, 0.0 us)
Async XLA Ops:
  6.0 11.4 %copy-start.1 = (bf16[128,1408]{1,0:T(8,128)(2,1)S(1)}, bf16[128,1408]{1,0:T(8,128)(2,1)}, u32[]{:S(2)}) copy-start(bf16[128,1408]{1,0:T(8,128)(2,1)} %param.17) | copy-start | bytes 1081348
  6.0 11.9 %copy-start.2 = (bf16[128,1408]{1,0:T(8,128)(2,1)S(1)}, bf16[128,1408]{1,0:T(8,128)(2,1)}, u32[]{:S(2)}) copy-start(bf16[128,1408]{1,0:T(8,128)(2,1)} %param.18) | copy-start | bytes 1081348
  17.4 2.3 copy-start.3
  178.6 30.9 %copy-start = (bf16[2048,288]{0,1:T(8,128)(2,1)S(1)}, bf16[2048,288]{0,1:T(8,128)(2,1)}, u32[]{:S(2)}) copy-start(bf16[2048,288]{0,1:T(8,128)(2,1)} %param.21) | copy-start | bytes 3538948

commit v2 on v1

--- a/solution.py
+++ b/solution.py
@@ -215,17 +215,15 @@
     return v / (1.0 + jnp.exp(-v))
 
 
-def expert_kernel(n_exp, experts, in_cols, out_cols, tok_ref, gu_ref, dn_ref, part_ref):
-    dp, ex, _ = position()
-    width = gu_ref.shape[0]
-    mine = dp * n_exp + ex
-    rows = tok_ref.shape[0]
+def expert_tile(mine, experts, in_cols, out_cols, tok, gu, dn):
+    width = gu.shape[0]
+    rows = tok.shape[0]
     lane = lax.broadcasted_iota(jnp.int32, (rows, LANES), 1)
-    extra = tok_ref[:, width:].astype(jnp.float32)
+    extra = tok[:, width:].astype(jnp.float32)
     weight = jnp.sum(
         jnp.where((lane == mine) | (lane == mine + experts), extra, 0.0), axis=1, keepdims=True
     )
-    hid = jnp.dot(tok_ref[:, :width], gu_ref[...], preferred_element_type=jnp.float32)
+    hid = jnp.dot(tok[:, :width], gu[...], preferred_element_type=jnp.float32)
     main = out_cols - LANES
     act = silu(hid[:, :main]) * hid[:, main : 2 * main] * weight
     mixed = hid[:, 2 * main : in_cols]
@@ -234,27 +232,9 @@
     span = (hid.shape[1] - in_cols) // 2
     shared = silu(hid[:, in_cols : in_cols + span]) * hid[:, in_cols + span :]
     acts = jnp.concatenate([act, mixed_act, shared], axis=1).astype(jnp.bfloat16)
-    part_ref[...] = lax.dot_general(
-        acts, dn_ref[...], (((1,), (1,)), ((), ())), preferred_element_type=jnp.float32
-    ).astype(jnp.bfloat16)
-
-
-def expert_dense(n_exp, experts, in_cols, out_cols, tok, gu, dn):
-    total, wide = tok.shape
-    width = gu.shape[0]
-    tile = 256
-    return pl.pallas_call(
-        functools.partial(expert_kernel, n_exp, experts, in_cols, out_cols),
-        grid=(total // tile,),
-        in_specs=[
-            pl.BlockSpec((tile, wide), lambda i: (i, 0)),
-            pl.BlockSpec(gu.shape, lambda i: (0, 0)),
-            pl.BlockSpec(dn.shape, lambda i: (0, 0)),
-        ],
-        out_specs=pl.BlockSpec((tile, width), lambda i: (i, 0)),
-        out_shape=jax.ShapeDtypeStruct((total, width), jnp.bfloat16),
-        compiler_params=pltpu.CompilerParams(vmem_limit_bytes=VMEM_BYTES),
-    )(tok, gu, dn)
+    return lax.dot_general(
+        acts, dn[...], (((1,), (1,)), ((), ())), preferred_element_type=jnp.float32
+    )
 
 
 def scale_rows(wide, gain):
@@ -266,13 +246,28 @@
     return (one.astype(jnp.float32) + other.astype(jnp.float32)).astype(jnp.bfloat16)
 
 
-def reduce_kernel(
-    n_dp, n_exp, part, hidden, gain, kv_w, layer, kv,
-    r1, s1, r2x, r2y, s2, r3, s3, r4, rows_own, rows_peer,
-    c_s, c_r, x_s, x_r, y_s, y_r, b_s, b_r, z_s, z_r, k_s, k_r,
+def expert_reduce_kernel(
+    n_dp, n_exp, experts, in_cols, out_cols,
+    tok_hbm, gu_hbm, dn_hbm, hidden, gain, kv_w, layer, kv,
+    tok, gu, dn, pm, r1, s1, r2x, r2y, s2, r3, s3, r4, rows_own, rows_peer,
+    local, c_s, c_r, x_s, x_r, y_s, y_r, b_s, b_r, z_s, z_r, k_s, k_r,
 ):
     dp, ex, mp = position()
     block = hidden.shape[0]
+    half = n_dp // 2
+    order = [d for pair in zip(range(half), range(half, n_dp)) for d in pair]
+    chunk = tok.shape[1]
+
+    loads = {}
+    for at, (name, src, dst) in enumerate(
+        [("gu", gu_hbm, gu), (order[0], None, None), ("dn", dn_hbm, dn)]
+        + [(d, None, None) for d in order[1:]]
+    ):
+        if src is None:
+            src, dst = tok_hbm.at[pl.ds(name * chunk, chunk)], tok.at[name]
+        loads[name] = pltpu.make_async_copy(src, dst, local.at[at])
+        loads[name].start()
+
     y, core = ex // 2, lax.rem(ex, 2)
     mate = (dp, ex + 1 - 2 * core, mp)
     xpeer = (dp, ex, 1 - mp)
@@ -281,73 +276,99 @@
     barrier([mate, xpeer, ypeer] + zpeers)
     started = []
 
-    def send(src, dst, s, r, to):
-        copy = pltpu.make_async_remote_copy(
+    def remote(src, dst, s, r, to):
+        return pltpu.make_async_remote_copy(
             src_ref=src, dst_ref=dst, send_sem=s, recv_sem=r, device_id=to, device_id_type=MESH
         )
+
+    def send(src, dst, s, r, to):
+        copy = remote(src, dst, s, r, to)
         copy.start()
         started.append(copy)
         return copy
 
-    half = n_dp // 2
-    order = [g for pair in zip(range(half), range(half, n_dp)) for g in pair]
-
-    def pair_rows(group, c):
-        index = (group // 2 * n_exp + group % 2 * 2 + c) * 2
-        return pl.ds(pl.multiple_of(index * block, 2 * block), 2 * block)
-
-    from_mate = {}
-    for d in order:
-        for g in (2 * d, 2 * d + 1):
-            from_mate[g] = send(
-                part.at[pair_rows(g, 1 - core)], r1.at[g], c_s.at[g], c_r.at[g], mate
+    def tile(d, c):
+        pairs = [
+            tok[d, pl.ds(pl.multiple_of((4 * j + 2 * c) * block, 2 * block), 2 * block), :]
+            for j in range(2)
+        ]
+        return expert_tile(
+            dp * n_exp + ex, experts, in_cols, out_cols, jnp.concatenate(pairs, axis=0), gu, dn
+        )
+
+    def part_rows(j, m, count):
+        return pl.ds(pl.multiple_of((2 * j + m) * block, block), count * block)
+
+    first_x, first_y, second = {}, {}, {}
+
+    def compute(d):
+        loads[d].wait()
+        pm[d] = tile(d, 1 - core).astype(jnp.bfloat16)
+        from_mate = send(pm.at[d], r1.at[d], c_s.at[d], c_r.at[d], mate)
+        own = tile(d, core)
+        from_mate.wait_recv()
+        s1[d] = (own + r1[d].astype(jnp.float32)).astype(jnp.bfloat16)
+        if d < half:
+            for j in range(2):
+                g = 2 * d + j
+                first_x[g] = send(
+                    s1.at[d, part_rows(j, 1 - mp, 1)], r2x.at[g], x_s.at[g], x_r.at[g], xpeer
+                )
+        else:
+            at = d - half
+            first_y[d] = send(
+                s1.at[d, part_rows(1 - y, 0, 2)], r2y.at[at], y_s.at[at], y_r.at[at], ypeer
             )
-    mine = pl.ds(pl.multiple_of(mp * block, block), block)
-    theirs = pl.ds(pl.multiple_of((1 - mp) * block, block), block)
-    first_x, first_y = {}, {}
-    for d in order:
-        for g in (2 * d, 2 * d + 1):
-            from_mate[g].wait_recv()
-            s1[g] = add(part[pair_rows(g, core), :], r1[g])
-            if d < half:
-                first_x[g] = send(s1.at[g, theirs], r2x.at[g], x_s.at[g], x_r.at[g], xpeer)
-        if d >= half:
-            first_y[d] = send(
-                s1.at[2 * d + 1 - y], r2y.at[d - half], y_s.at[d - half], y_r.at[d - half], ypeer
-            )
-    second = {}
-    for d in order:
+
+    def second_stage(d):
         if d < half:
             for j in range(2):
                 g = 2 * d + j
                 first_x[g].wait_recv()
-                s2[d, j] = add(s1[g, mine, :], r2x[g])
+                s2[d, j] = add(s1[d, part_rows(j, mp, 1), :], r2x[g])
             second[d] = send(s2.at[d, 1 - y], r3.at[d], b_s.at[d], b_r.at[d], ypeer)
         else:
             first_y[d].wait_recv()
-            both = add(s1[2 * d + y], r2y[d - half])
+            both = add(s1[d, part_rows(y, 0, 2), :], r2y[d - half])
             s2[d, 0] = both[:block]
             s2[d, 1] = both[block:]
             second[d] = send(s2.at[d, 1 - mp], r3.at[d], b_s.at[d], b_r.at[d], xpeer)
-    for d in order:
+
+    def to_z(d):
+        return remote(s3.at[d], r4.at[dp], z_s.at[d], z_r.at[dp], (d, ex, mp))
+
+    def third_stage(d):
         second[d].wait_recv()
         s3[d] = add(s2[d, y if d < half else mp], r3[d])
-    third = []
-    for k in range(1, n_dp):
-        third.append(
-            send(
-                s3.at[lax.rem(dp + k, n_dp)], r4.at[k - 1], z_s.at[k - 1], z_r.at[k - 1],
-                zpeers[k - 1],
-            )
-        )
+
+        @pl.when(dp != d)
+        def _():
+            to_z(d).start()
+
+    loads["gu"].wait()
+    loads["dn"].wait()
+    lag = 2
+    for at, d in enumerate(order):
+        compute(d)
+        if at >= lag:
+            second_stage(order[at - lag])
+    for at in range(max(0, n_dp - lag), n_dp):
+        second_stage(order[at])
+        third_stage(order[at - n_dp + lag])
+    for at in range(lag, n_dp):
+        third_stage(order[at])
+
     total = hidden[...].astype(jnp.float32) + s3[dp].astype(jnp.float32)
     for k in range(1, n_dp):
-        third[k - 1].wait_recv()
-        total = total + r4[k - 1].astype(jnp.float32)
+        other = lax.rem(dp + k, n_dp)
+        remote(s3.at[other], r4.at[other], z_s.at[other], z_r.at[other], zpeers[k - 1]).wait_recv()
+        total = total + r4[other].astype(jnp.float32)
     layer_rows = total.astype(jnp.bfloat16)
     layer[...] = layer_rows
     rows_own[...] = scale_rows(layer_rows.astype(jnp.float32), gain[...])
     last = send(rows_own, rows_peer, k_s.at[0], k_r.at[0], xpeer)
+    mine = pl.ds(pl.multiple_of(mp * block, block), block)
+    theirs = pl.ds(pl.multiple_of((1 - mp) * block, block), block)
     kv[mine, :] = jnp.dot(
         rows_own[...], kv_w[...], preferred_element_type=jnp.float32
     ).astype(jnp.bfloat16)
@@ -357,28 +378,38 @@
     ).astype(jnp.bfloat16)
     for copy in started:
         copy.wait_send()
-
-
-def reduce_tail(n_dp, n_exp, part, hidden, gain, kv_w):
+    for d in range(n_dp):
+
+        @pl.when(dp != d)
+        def _(d=d):
+            to_z(d).wait_send()
+
+
+def expert_reduce(n_dp, n_exp, experts, in_cols, out_cols, tok, gu, dn, hidden, gain, kv_w):
     block, width = hidden.shape
     half = n_dp // 2
     bf16 = jnp.bfloat16
     shapes = [
-        (2 * n_dp, 2 * block, width),
-        (2 * n_dp, 2 * block, width),
+        (n_dp, tok.shape[0] // n_dp, tok.shape[1]),
+        gu.shape,
+        dn.shape,
+        (n_dp, 4 * block, width),
+        (n_dp, 4 * block, width),
+        (n_dp, 4 * block, width),
         (2 * half, block, width),
         (half, 2 * block, width),
         (n_dp, 2, block, width),
         (n_dp, block, width),
         (n_dp, block, width),
-        (n_dp - 1, block, width),
+        (n_dp, block, width),
         (block, width),
         (block, width),
     ]
-    counts = [2 * n_dp] * 2 + [2 * half] * 2 + [half] * 2 + [n_dp] * 2 + [n_dp - 1] * 2 + [1] * 2
+    counts = [n_dp + 2] + [n_dp] * 2 + [2 * half] * 2 + [half] * 2 + [n_dp] * 4 + [1] * 2
     return pl.pallas_call(
-        functools.partial(reduce_kernel, n_dp, n_exp),
-        in_specs=[pl.BlockSpec(memory_space=pltpu.VMEM)] * 4,
+        functools.partial(expert_reduce_kernel, n_dp, n_exp, experts, in_cols, out_cols),
+        in_specs=[pl.BlockSpec(memory_space=pl.ANY)] * 3
+        + [pl.BlockSpec(memory_space=pltpu.VMEM)] * 3,
         out_specs=[pl.BlockSpec(memory_space=pltpu.VMEM)] * 2,
         out_shape=[
             jax.ShapeDtypeStruct((block, width), bf16),
@@ -389,7 +420,7 @@
         compiler_params=pltpu.CompilerParams(
             collective_id=1, has_side_effects=True, vmem_limit_bytes=VMEM_BYTES
         ),
-    )(part, hidden, gain, kv_w)
+    )(tok, gu, dn, hidden, gain, kv_w)
 
 
 def pieces_of(weights, groups):
@@ -435,8 +466,12 @@
     s_in = jnp.concatenate([pieces_of(shared_gate, groups), pieces_of(shared_up, groups)], axis=2)
     s_out = pieces_of(shared_down, groups)
     every, gu, dn = gather(n_dp, n_exp, tok, w_in, w_out, s_in, s_out)
-    part = expert_dense(n_exp, experts, w_in.shape[2], w_out.shape[2], every, gu, dn)
-    return tuple(reduce_tail(n_dp, n_exp, part, hidden, next_gain[None, :], kv_weight))
+    return tuple(
+        expert_reduce(
+            n_dp, n_exp, experts, w_in.shape[2], w_out.shape[2],
+            every, gu, dn, hidden, next_gain[None, :], kv_weight,
+        )
+    )
 
 
 def dense_fits(mesh, hidden, expert_in, expert_ids):

time: 294 us -> 267 us (0.908); the launches traced: 294 us -> 262 us
  Pallas kernels: 279 us -> 248 us
    pallas_call x2 -> x1, Pallas kernels: 110 us -> 78.8 us  [expert_reduce(): pl.pallas_call(functools.partial(expert_reduce_kernel, n_dp, n_exp, exper...]
where the time goes in v2:
time: 267 us; the launch traced here: 262 us
  Pallas kernels  248 us (93%)
  local copies, waits for them, and re-layouts  8.38 us (3%)
  other arithmetic  5.52 us (2%)
    pallas_call x1, Pallas kernels, gather(): pl.pallas_call(functools.partial(gather_kernel, n_dp, n_exp), in_specs=[p...  157 us
    pallas_call x1, Pallas kernels, expert_reduce(): pl.pallas_call(functools.partial(expert_reduce_kernel, n_dp, n_exp, exper...  78.8 us
    pallas_call x1, Pallas kernels, pack(): pl.pallas_call(pack_kernel, grid=(local_e, rows // tile), in_specs=[pl.Bl...  11.3 us

profile of v2, /device:TPU:8, one launch (start us, length us, event | category | flops | bytes accessed | tf_op | source)
XLA Modules:
  0.0 262.3 jit_solution(18300401932175095025)
XLA Ops:
  0.6 0.7 convert_reduce_fusion
  1.3 0.7 convert_divide_fusion
  2.0 0.7 select_reduce_fusion
  2.7 0.1 copy.37
  2.8 0.1 copy.38
  2.9 1.1 fusion.3
  4.0 1.1 fusion.5
  5.1 0.8 concatenate.6.tok
  6.0 0.0 copy-start.1
  6.0 0.0 copy-start.2
  6.0 11.3 %shard_map.122 = (bf16[8,256,1408]{2,1,0:T(8,128)(2,1)}, bf16[8,256,768]{2,1,0:T(8,128)(2,1)}) custom-call(f32[4,256,2816]{2,1,0:T(8,128)} %in_ref.1, f32[4,256,1408]{2,1,0:T(8,128)} %out_ref.1), custom_call_target="tpu_custom_call" | custom-call | tf_op jit(solution)/shard_map/pallas_call | solution.py:52
  17.3 0.0 copy-done.1
  17.3 0.2 copy.40
  17.6 0.0 copy-start.3
  17.6 0.3 copy.41
  17.9 0.0 copy-done.2
  17.9 0.2 copy.42
  18.1 0.3 copy.43
  18.4 1.2 fusion.2.s_in
  19.6 0.0 copy-done.3
  19.6 0.2 copy.44
  19.8 0.3 copy.45
  20.1 1.0 pad.12.s_out
  21.1 0.0 copy-start
  21.1 157.5 %shard_map.123 = (bf16[2048,2176]{1,0:T(8,128)(2,1)}, bf16[2048,1664]{1,0:T(8,128)(2,1)}, bf16[2048,896]{1,0:T(8,128)(2,1)}) custom-call(bf16[64,2176]{1,0:T(8,128)(2,1)} %concatenate.6.tok, bf16[8,256,1408]{2,1,0:T(8,128)(2,1)} %get-tuple-element.7.w_in, bf16[8,256,768]{2,1,0:T(8,128)(2,1)} %get-tuple-element.8.w_out, bf16[16,128,256]{2,1,0:T(8,128)(2,1)} %fusion.2.s_in, ...), custom_call_target="tpu_custom_call" | custom-call | tf_op jit(solution)/shard_map/pallas_call | solution.py:198
  178.6 0.0 copy-done
  178.6 1.6 copy.46.kv_w
  180.2 78.8 %shard_map.124 = (bf16[64,2048]{1,0:T(8,128)(2,1)}, bf16[128,288]{1,0:T(8,128)(2,1)}) custom-call(bf16[2048,2176]{1,0:T(8,128)(2,1)} %get-tuple-element.9.tok_hbm, bf16[2048,1664]{1,0:T(8,128)(2,1)} %get-tuple-element.10.gu_hbm, bf16[2048,896]{1,0:T(8,128)(2,1)} %get-tuple-element.11.dn_hbm, bf16[64,2048]{1,0:T(8,128)(2,1)} %hidden.1, f32[1,2048]{1,0:T(1,128)} %bitcast.13, ...), custom_call_target="tpu_custom_call" | custom-call | tf_op jit(solution)/shard_map/pallas_call | solution.py:409
  259.0 1.6 copy.47
  260.6 1.7 copy.49
  (4 shorter events, 0.0 us)
Async XLA Ops:
  6.0 11.4 %copy-start.1 = (bf16[128,1408]{1,0:T(8,128)(2,1)S(1)}, bf16[128,1408]{1,0:T(8,128)(2,1)}, u32[]{:S(2)}) copy-start(bf16[128,1408]{1,0:T(8,128)(2,1)} %param.17) | copy-start | bytes 1081348
  6.0 11.9 %copy-start.2 = (bf16[128,1408]{1,0:T(8,128)(2,1)S(1)}, bf16[128,1408]{1,0:T(8,128)(2,1)}, u32[]{:S(2)}) copy-start(bf16[128,1408]{1,0:T(8,128)(2,1)} %param.18) | copy-start | bytes 1081348
  17.6 2.0 copy-start.3
  21.1 157.5 %copy-start = (bf16[2048,288]{0,1:T(8,128)(2,1)S(1)}, bf16[2048,288]{0,1:T(8,128)(2,1)}, u32[]{:S(2)}) copy-start(bf16[2048,288]{0,1:T(8,128)(2,1)} %param.21) | copy-start | bytes 3538948

commit v3 on v2

--- a/solution.py
+++ b/solution.py
@@ -23,59 +23,37 @@
     pl.semaphore_wait(sem, len(peers))
 
 
-def pack_kernel(in_ref, out_ref, in_pack, out_pack):
-    rows, full = out_ref.shape[1:]
+def pack_piece(e, wide_in, wide_out, in_pack, out_pack):
+    rows, full = wide_out.shape[1:]
     main = full // (2 * LANES) * LANES
     mid = main + LANES
     half = LANES // 2
     low = lax.broadcasted_iota(jnp.int32, (rows, LANES), 1) < half
-    for first, core in ((0, 0), (mid, 1)):
-        in_pack[core, :, :main] = in_ref[0, :, first : first + main].astype(jnp.bfloat16)
-        in_pack[core, :, main : 2 * main] = in_ref[
-            0, :, full + first : full + first + main
-        ].astype(jnp.bfloat16)
-        out_pack[core, :, :main] = out_ref[0, :, first : first + main].astype(jnp.bfloat16)
-    gate = in_ref[0, :, main:mid]
-    up = in_ref[0, :, full + main : full + mid]
-    down = out_ref[0, :, main:mid]
-    in_pack[0, :, 2 * main :] = jnp.where(low, gate, pltpu.roll(up, half, 1)).astype(jnp.bfloat16)
-    in_pack[1, :, 2 * main :] = jnp.where(low, pltpu.roll(gate, half, 1), up).astype(jnp.bfloat16)
-    out_pack[0, :, main:] = jnp.where(low, down, 0.0).astype(jnp.bfloat16)
-    out_pack[1, :, main:] = jnp.where(low, pltpu.roll(down, half, 1), 0.0).astype(jnp.bfloat16)
-
-
-def pack(expert_in, expert_out):
-    local_e, rows, double = expert_in.shape
-    full = double // 2
-    wide = (full // (2 * LANES) + 1) * LANES
-    tile = 128
-    return pl.pallas_call(
-        pack_kernel,
-        grid=(local_e, rows // tile),
-        in_specs=[
-            pl.BlockSpec((1, tile, double), lambda e, i: (e, i, 0)),
-            pl.BlockSpec((1, tile, full), lambda e, i: (e, i, 0)),
-        ],
-        out_specs=[
-            pl.BlockSpec((2, tile, full), lambda e, i: (e, i, 0)),
-            pl.BlockSpec((2, tile, wide), lambda e, i: (e, i, 0)),
-        ],
-        out_shape=[
-            jax.ShapeDtypeStruct((2 * local_e, rows, full), jnp.bfloat16),
-            jax.ShapeDtypeStruct((2 * local_e, rows, wide), jnp.bfloat16),
-        ],
-        compiler_params=pltpu.CompilerParams(vmem_limit_bytes=VMEM_BYTES),
-    )(expert_in, expert_out)
+    bf16 = jnp.bfloat16
+    for first, side in ((0, 0), (mid, 1)):
+        in_pack[e, side, :, :main] = wide_in[e, :, first : first + main].astype(bf16)
+        in_pack[e, side, :, main : 2 * main] = wide_in[
+            e, :, full + first : full + first + main
+        ].astype(bf16)
+        out_pack[e, side, :, :main] = wide_out[e, :, first : first + main].astype(bf16)
+    gate = wide_in[e, :, main:mid]
+    up = wide_in[e, :, full + main : full + mid]
+    down = wide_out[e, :, main:mid]
+    in_pack[e, 0, :, 2 * main :] = jnp.where(low, gate, pltpu.roll(up, half, 1)).astype(bf16)
+    in_pack[e, 1, :, 2 * main :] = jnp.where(low, pltpu.roll(gate, half, 1), up).astype(bf16)
+    out_pack[e, 0, :, main:] = jnp.where(low, down, 0.0).astype(bf16)
+    out_pack[e, 1, :, main:] = jnp.where(low, pltpu.roll(down, half, 1), 0.0).astype(bf16)
 
 
 def gather_kernel(
-    n_dp, n_exp, tok, w_in, w_out, s_in, s_out, all_tok, gu, dn,
+    n_dp, n_exp, tok, expert_in, expert_out, s_in, s_out, all_tok, gu, dn,
+    wide_in, wide_out, w_in, w_out,
     z_s, z_r, h_s, h_r, f_s, f_r, win_s, win_r, wout_s, wout_r, sin_s, sin_r, sout_s, sout_r, local,
 ):
     dp, ex, mp = position()
     block = tok.shape[0]
-    in_cols, out_cols = w_in.shape[2], w_out.shape[2]
-    w_rows, s_rows = w_in.shape[1], s_in.shape[1]
+    in_cols, out_cols = w_in.shape[3], w_out.shape[3]
+    w_rows, s_rows = w_in.shape[2], s_in.shape[1]
     mate = (dp, ex + 1 - 2 * lax.rem(ex, 2), mp)
     xpeer = (dp, ex, 1 - mp)
     ypeer = (dp, lax.rem(ex + n_exp // 2, n_exp), mp)
@@ -92,6 +70,15 @@
     def in_column(a, b):
         return (lax.rem(dp + a, n_dp), lax.rem(ex + b, n_exp), mp)
 
+    y_ex = ypeer[1]
+    targets = [y_ex, ex, lax.rem(mate[1] + n_exp // 2, n_exp), mate[1]]
+    loads = []
+    for kind, e in enumerate(targets):
+        for src, dst, at in ((expert_in, wide_in, 3), (expert_out, wide_out, 4)):
+            copy = pltpu.make_async_copy(src.at[e], dst.at[e], local.at[at + 2 * kind])
+            copy.start()
+            loads.append(copy)
+
     barrier(
         [in_plane(a, b) for a, b in plane] + [in_column(a, b) for a, b in column if a != 0]
     )
@@ -132,46 +119,62 @@
     s_at = pl.ds(pl.multiple_of((dp * n_exp + ex) * s_rows, s_rows), s_rows)
     rest = []
     locals_ = [own]
-    pieces = (
-        (w_in, gu.at[w_at, pl.ds(0, in_cols)], ex * 2 + mp),
-        (w_out, dn.at[w_at, pl.ds(0, out_cols)], ex * 2 + mp),
-        (s_in, gu.at[s_at, pl.ds(in_cols, s_in.shape[2])], dp * n_exp + ex),
-        (s_out, dn.at[s_at, pl.ds(out_cols, s_out.shape[2])], dp * n_exp + ex),
-    )
-    for at, (src, dst, index) in enumerate(pieces):
-        copy = pltpu.make_async_copy(src.at[index], dst, local.at[1 + at])
+    gu_at, dn_at = gu.at[w_at, pl.ds(0, in_cols)], dn.at[w_at, pl.ds(0, out_cols)]
+    gu_s = gu.at[s_at, pl.ds(in_cols, s_in.shape[2])]
+    dn_s = dn.at[s_at, pl.ds(out_cols, s_out.shape[2])]
+
+    def keep(src, dst, at):
+        copy = pltpu.make_async_copy(src, dst, local.at[at])
         copy.start()
         locals_.append(copy)
-    for at, (a, b) in enumerate(plane):
-        to = in_plane(a, b)
-        index = to[1] * 2 + to[2]
-        rest.append(send(w_in.at[index], pieces[0][1], win_s.at[at], win_r.at[at], to))
-        rest.append(send(w_out.at[index], pieces[1][1], wout_s.at[at], wout_r.at[at], to))
+
+    def weights(kind):
+        e = targets[kind]
+        loads[2 * kind].wait()
+        loads[2 * kind + 1].wait()
+        pack_piece(e, wide_in, wide_out, w_in, w_out)
+        for b in range(2):
+            m = lax.rem(mp + b, 2)
+            at = 2 * kind + b
+            if kind == 1 and b == 0:
+                keep(w_in.at[e, m], gu_at, 3 + 2 * n_exp)
+                keep(w_out.at[e, m], dn_at, 4 + 2 * n_exp)
+                continue
+            to = (dp, e, m)
+            rest.append(send(w_in.at[e, m], gu_at, win_s.at[at], win_r.at[at], to))
+            rest.append(send(w_out.at[e, m], dn_at, wout_s.at[at], wout_r.at[at], to))
+
+    weights(0)
+    keep(s_in.at[dp * n_exp + ex], gu_s, 1)
+    keep(s_out.at[dp * n_exp + ex], dn_s, 2)
     for at, (a, b) in enumerate(column):
         to = in_column(a, b)
         index = to[0] * n_exp + to[1]
-        rest.append(send(s_in.at[index], pieces[2][1], sin_s.at[at], sin_r.at[at], to))
-        rest.append(send(s_out.at[index], pieces[3][1], sout_s.at[at], sout_r.at[at], to))
+        rest.append(send(s_in.at[index], gu_s, sin_s.at[at], sin_r.at[at], to))
+        rest.append(send(s_out.at[index], dn_s, sout_s.at[at], sout_r.at[at], to))
+    weights(1)
 
     for k in range(1, n_dp):
         from_z[k].wait_recv()
         spread(k, all_tok.at[rows_of(k, ex, mp)])
+    weights(2)
+    weights(3)
     from_f = {}
 
     def forward(kind, k, rows, to):
         at = kind * n_dp + k
         from_f[kind, k] = send(all_tok.at[rows], all_tok.at[rows], f_s.at[at], f_r.at[at], to)
 
-    y_ex = ypeer[1]
+    over_y = n_dp // 4
     for k in range(n_dp):
         from_h[0, k].wait_recv()
         rows = rows_of(k, ex, 1 - mp)
-        if k < n_dp // 2:
+        if k < over_y:
             forward(0, k, rows, ypeer)
         forward(1, k, rows, mate)
         from_h[1, k].wait_recv()
         rows = rows_of(k, y_ex, mp)
-        if k >= n_dp // 2:
+        if k >= over_y:
             forward(0, k, rows, xpeer)
         forward(2, k, rows, mate)
     for k in range(n_dp):
@@ -189,26 +192,35 @@
         copy.wait()
 
 
-def gather(n_dp, n_exp, tok, w_in, w_out, s_in, s_out):
+def gather(n_dp, n_exp, tok, expert_in, expert_out, s_in, s_out):
     total = tok.shape[0] * n_dp * n_exp * 2
-    depth = w_in.shape[1] * n_exp * 2
-    n_plane, n_column = n_exp * 2 - 1, n_dp * n_exp - 1
+    local_e, rows, full = expert_out.shape
+    depth = rows * n_exp * 2
+    wide = (full // (2 * LANES) + 1) * LANES
+    n_plane, n_column = n_exp * 2, n_dp * n_exp - 1
     counts = [n_dp] * 2 + [3 * n_dp] * 2 + [4 * n_dp] * 2
-    counts += [n_plane] * 4 + [n_column] * 4 + [5]
+    counts += [n_plane] * 4 + [n_column] * 4 + [5 + 2 * n_exp]
+    bf16 = jnp.bfloat16
     return pl.pallas_call(
         functools.partial(gather_kernel, n_dp, n_exp),
         in_specs=[pl.BlockSpec(memory_space=pl.ANY)] * 5,
         out_specs=[pl.BlockSpec(memory_space=pl.ANY)] * 3,
         out_shape=[
-            jax.ShapeDtypeStruct((total, tok.shape[1]), jnp.bfloat16),
-            jax.ShapeDtypeStruct((depth, w_in.shape[2] + s_in.shape[2]), jnp.bfloat16),
-            jax.ShapeDtypeStruct((depth, w_out.shape[2] + s_out.shape[2]), jnp.bfloat16),
+            jax.ShapeDtypeStruct((total, tok.shape[1]), bf16),
+            jax.ShapeDtypeStruct((depth, full + s_in.shape[2]), bf16),
+            jax.ShapeDtypeStruct((depth, wide + s_out.shape[2]), bf16),
         ],
-        scratch_shapes=[pltpu.SemaphoreType.DMA((count,)) for count in counts],
+        scratch_shapes=[
+            pltpu.VMEM(expert_in.shape, jnp.float32),
+            pltpu.VMEM(expert_out.shape, jnp.float32),
+            pltpu.VMEM((local_e, 2, rows, full), bf16),
+            pltpu.VMEM((local_e, 2, rows, wide), bf16),
+        ]
+        + [pltpu.SemaphoreType.DMA((count,)) for count in counts],
         compiler_params=pltpu.CompilerParams(
             collective_id=0, has_side_effects=True, vmem_limit_bytes=VMEM_BYTES
         ),
-    )(tok, w_in, w_out, s_in, s_out)
+    )(tok, expert_in, expert_out, s_in, s_out)
 
 
 def silu(v):
@@ -446,7 +458,6 @@
     n_dp, n_exp = lax.axis_size("dp"), lax.axis_size("expert")
     groups = n_dp * n_exp
     experts = expert_in.shape[0] * n_dp
-    w_in, w_out = pack(expert_in, expert_out)
     normed = scale_rows(hidden.astype(jnp.float32), norm_gain)
     levels = gate_levels.astype(jnp.float32)
     gate_weights = levels / jnp.sum(levels, axis=1, keepdims=True)
@@ -465,10 +476,11 @@
     )
     s_in = jnp.concatenate([pieces_of(shared_gate, groups), pieces_of(shared_up, groups)], axis=2)
     s_out = pieces_of(shared_down, groups)
-    every, gu, dn = gather(n_dp, n_exp, tok, w_in, w_out, s_in, s_out)
+    every, gu, dn = gather(n_dp, n_exp, tok, expert_in, expert_out, s_in, s_out)
+    in_cols, out_cols = gu.shape[1] - s_in.shape[2], dn.shape[1] - s_out.shape[2]
     return tuple(
         expert_reduce(
-            n_dp, n_exp, experts, w_in.shape[2], w_out.shape[2],
+            n_dp, n_exp, experts, in_cols, out_cols,
             every, gu, dn, hidden, next_gain[None, :], kv_weight,
         )
     )

time: 267 us -> 252 us (0.944)
  Pallas kernels: 248 us -> 231 us
    pallas_call x1 -> x0, Pallas kernels: 11.3 us -> none  [pack(): pl.pallas_call(pack_kernel, grid=(local_e, rows // tile), in_specs=[pl.Bl...]
    pallas_call x1, Pallas kernels: 157 us -> 154 us  [gather(): pl.pallas_call(functools.partial(gather_kernel, n_dp, n_exp), in_specs=[p...]
where the time goes in v3:
time: 252 us; the launch traced here: 247 us
  Pallas kernels  231 us (92%)
  local copies, waits for them, and re-layouts  9.31 us (4%)
  other arithmetic  5.61 us (2%)
    pallas_call x1, Pallas kernels, gather(): pl.pallas_call(functools.partial(gather_kernel, n_dp, n_exp), in_specs=[p...  154 us
    pallas_call x1, Pallas kernels, expert_reduce(): pl.pallas_call(functools.partial(expert_reduce_kernel, n_dp, n_exp, exper...  76.4 us

profile of v3, /device:TPU:8, one launch (start us, length us, event | category | flops | bytes accessed | tf_op | source)
XLA Modules:
  0.0 246.5 jit_solution(8341212528230198074)
XLA Ops:
  0.6 0.0 copy-start.1
  0.6 0.8 convert_reduce_fusion
  1.4 0.7 convert_divide_fusion
  2.1 0.7 select_reduce_fusion
  2.8 0.1 copy.37
  2.9 0.1 copy.38
  3.0 1.1 fusion.3
  4.1 1.1 fusion.5
  5.2 0.8 concatenate.6.tok
  6.0 1.2 copy.40
  7.2 0.0 copy-start.2
  7.2 0.3 copy.41
  7.5 0.0 copy-done.1
  7.5 0.2 copy.42
  7.7 0.3 copy.43
  8.0 1.2 fusion.2.s_in
  9.3 0.0 copy-done.2
  9.3 0.2 copy.44
  9.5 0.3 copy.45
  9.8 1.0 pad.12.s_out
  10.8 0.0 copy-start
  10.8 154.5 %shard_map.122 = (bf16[2048,2176]{1,0:T(8,128)(2,1)}, bf16[2048,1664]{1,0:T(8,128)(2,1)}, bf16[2048,896]{1,0:T(8,128)(2,1)}) custom-call(bf16[64,2176]{1,0:T(8,128)(2,1)} %concatenate.6.tok, f32[4,256,2816]{2,1,0:T(8,128)} %expert_in.1, f32[4,256,1408]{2,1,0:T(8,128)} %expert_out.1, bf16[16,128,256]{2,1,0:T(8,128)(2,1)} %fusion.2.s_in, ...), custom_call_target="tpu_custom_call" | custom-call | tf_op jit(solution)/shard_map/pallas_call | solution.py:204
  165.2 0.0 copy-done
  165.3 1.6 copy.46.kv_w
  166.8 76.4 %shard_map.123 = (bf16[64,2048]{1,0:T(8,128)(2,1)}, bf16[128,288]{1,0:T(8,128)(2,1)}) custom-call(bf16[2048,2176]{1,0:T(8,128)(2,1)} %get-tuple-element.5.tok_hbm, bf16[2048,1664]{1,0:T(8,128)(2,1)} %get-tuple-element.6.gu_hbm, bf16[2048,896]{1,0:T(8,128)(2,1)} %get-tuple-element.7.dn_hbm, bf16[64,2048]{1,0:T(8,128)(2,1)} %hidden.1, f32[1,2048]{1,0:T(1,128)} %bitcast.13, ...), custom_call_target="tpu_custom_call" | custom-call | tf_op jit(solution)/shard_map/pallas_call | solution.py:421
  243.2 1.6 copy.47
  244.9 1.7 copy.49
  (4 shorter events, 0.0 us)
Async XLA Ops:
  0.6 6.9 %copy-start.1 = (bf16[128,1408]{1,0:T(8,128)(2,1)S(1)}, bf16[128,1408]{1,0:T(8,128)(2,1)}, u32[]{:S(2)}) copy-start(bf16[128,1408]{1,0:T(8,128)(2,1)} %param.18) | copy-start | bytes 1081348
  7.2 2.1 copy-start.2
  10.8 154.5 %copy-start = (bf16[2048,288]{0,1:T(8,128)(2,1)S(1)}, bf16[2048,288]{0,1:T(8,128)(2,1)}, u32[]{:S(2)}) copy-start(bf16[2048,288]{0,1:T(8,128)(2,1)} %param.21) | copy-start | bytes 3538948
